TPU v7x, 32 devices: a whole 2x2x4 slice. The times are simulated.
32 devices in a mesh: rows: 8 (over y, x, core), cols: 4 (over z).
Axes of the slice: x: 2, y: 2, z: 4, core: 2. Of those that a mesh axis runs over, the one named last changes fastest.
Arguments:
- encoded: bfloat16 [256, 128, 384], P('rows', 'cols'), may hold values from -6 to 6
- conv_weight: bfloat16 [3, 3, 384, 384], replicated, may hold values from -0.109375 to 0.109375
- film_table: bfloat16 [360, 2, 384], replicated, may hold values from -3 to 3
- lead: int32 [1], replicated, may hold values from 0 to 359
Outputs:
- updated: bfloat16 [256, 128, 384], P('rows', 'cols')
All inputs are finite; a program needn't handle non-finite values.
Results may differ from a plain program's by a relative error of at most 0.006.
Values may be sent and summed in bfloat16 or wider, within the bound.
No kernel may reach another device: no remote copies, remote signals or barrier semaphores. Data moves between devices by JAX's collectives and lax.ppermute only.
A program may use at most 64 MiB of HBM per device.

v0:
```python
import jax
import jax.numpy as jnp
from jax import lax
from jax.sharding import PartitionSpec as P

DILATION_RATE = 128


def shifted(block, axis, distance):
    devices = range(lax.axis_size(axis))
    route = [(i - distance, i) for i in devices if i - distance in devices]
    return lax.ppermute(block, axis, route)


def tap_product(group, filter_kernel):
    count = group.shape[0]
    grid_height, grid_width, chans = (group.shape[1], group.shape[2], group.shape[3])
    flat = jnp.concatenate(
        [group[k].reshape(grid_height * grid_width, chans) for k in range(count)], axis=1
    )
    return jnp.dot(
        flat,
        filter_kernel.reshape(count * chans, filter_kernel.shape[-1]),
        preferred_element_type=jnp.float32,
    )


def local(encoded, conv_weight, film_table, lead):
    grid_height, grid_width, chans = encoded.shape
    active = jnp.maximum(encoded, jnp.zeros((), jnp.bfloat16))
    row_step = DILATION_RATE // grid_height
    column_step = DILATION_RATE // grid_width
    row_reach = row_step < lax.axis_size("rows")
    column_extent = column_step < lax.axis_size("cols")
    lower = shifted(active, "rows", row_step)
    upper = shifted(active, "rows", -row_step)
    middle = jnp.stack([lower, active, upper])
    total = tap_product(middle, conv_weight[:, 1])
    left = shifted(middle, "cols", column_step) if column_extent else jnp.zeros_like(middle)
    right = shifted(middle, "cols", -column_step) if column_extent else jnp.zeros_like(middle)
    total = total + tap_product(left, conv_weight[:, 0])
    total = total + tap_product(right, conv_weight[:, 2])
    leads = film_table.shape[0]
    onehot = (jnp.arange(leads, dtype=jnp.int32) == lead[0]).astype(jnp.bfloat16)[None]
    selected_taps = jnp.dot(
        onehot, film_table.reshape(leads, 2 * chans), preferred_element_type=jnp.float32
    )
    gamma = selected_taps[0, :chans]
    beta = selected_taps[0, chans:]
    conv = total.reshape(grid_height, grid_width, chans)
    updated = encoded.astype(jnp.float32) + conv * (1.0 + gamma) + beta
    return updated.astype(jnp.bfloat16)


def solution(mesh):
    placed = (P("rows", "cols", None), P(), P(), P())
    return jax.shard_map(
        local, mesh=mesh, in_specs=placed, out_specs=P("rows", "cols", None), check_vma=False
    )
```

profile of v0, /device:TPU:0, one launch (start us, length us, event | category | flops | bytes accessed | tf_op | source)
XLA Modules:
  0.0 29.8 jit_solution(11164703372075464590)
XLA Ops:
  0.0 0.0 copy-start.2
  0.0 0.0 copy-start.1
  0.0 1.4 %broadcast_maximum_fusion = bf16[32,32,384]{2,1,0:T(8,128)(2,1)S(1)} fusion(bf16[32,32,384]{2,1,0:T(8,128)(2,1)} %param.4), kind=kLoop, calls=%fused_computation.12 | loop fusion | flops 393216 | bytes 1572864 | tf_op jit(solution)/shard_map/max | solution.py:30
  1.4 4.9 %collective-permute-start = (bf16[32,32,384]{2,1,0:T(8,128)(2,1)S(1)}, bf16[32,32,384]{2,1,0:T(8,128)(2,1)S(1)}, u32[]{:S(2)}, u32[]{:S(2)}) collective-permute-start(bf16[32,32,384]{2,1,0:T(8,128)(2,1)S(1)} %broadcast_maximum_fusion), channel_id=1, source_target_pairs={{0,16},{4,20},{8,24},{12,28},{1,17},{5,21},{9,25},{13,29},{2,18},{... | collective-permute-start | bytes 2359304 | tf_op jit(solution)/shard_map/ppermute | solution.py:12
  6.3 1.3 %collective-permute-start.1 = (bf16[32,32,384]{2,1,0:T(8,128)(2,1)S(1)}, bf16[32,32,384]{2,1,0:T(8,128)(2,1)S(1)}, u32[]{:S(2)}, u32[]{:S(2)}) collective-permute-start(bf16[32,32,384]{2,1,0:T(8,128)(2,1)S(1)} %broadcast_maximum_fusion), channel_id=1, source_target_pairs={{16,0},{20,4},{24,8},{28,12},{17,1},{21,5},{25,9},{29,13},{18,2},{... | collective-permute-start | bytes 2359304 | tf_op jit(solution)/shard_map/ppermute | solution.py:12
  7.6 0.0 copy-done.2
  7.6 0.1 copy.5
  8.4 0.2 fusion.15
  8.6 0.0 copy-done.1
  8.6 0.3 fusion.14
  8.9 1.4 %fusion.10 = f32[1024,384]{1,0:T(8,128)S(1)} fusion(bf16[1152,384]{1,0:T(8,128)(2,1)S(1)} %bitcast.20, bf16[1152]{0:T(1024)(128)(2,1)S(1)} %concatenate.10), kind=kOutput, calls=%fused_computation.10 | convolution fusion | flops 905969664 | bytes 2459904 | tf_op jit(solution)/shard_map/dot_general | solution.py:21
  10.3 1.4 %fusion.8 = f32[1024,384]{1,0:T(8,128)S(1)} fusion(bf16[1152,384]{1,0:T(8,128)(2,1)S(1)} %bitcast.19, bf16[1152]{0:T(1024)(128)(2,1)S(1)} %concatenate.10), kind=kOutput, calls=%fused_computation.8 | convolution fusion | flops 905969664 | bytes 2459904 | tf_op jit(solution)/shard_map/dot_general | solution.py:21
  11.8 11.2 %collective-permute-done = bf16[32,32,384]{2,1,0:T(8,128)(2,1)S(1)} collective-permute-done((bf16[32,32,384]{2,1,0:T(8,128)(2,1)S(1)}, bf16[32,32,384]{2,1,0:T(8,128)(2,1)S(1)}, u32[]{:S(2)}, u32[]{:S(2)}) %collective-permute-start) | collective-permute-done | bytes 786464 | tf_op jit(solution)/shard_map/ppermute | solution.py:12
  23.0 4.2 %collective-permute-done.1 = bf16[32,32,384]{2,1,0:T(8,128)(2,1)S(1)} collective-permute-done((bf16[32,32,384]{2,1,0:T(8,128)(2,1)S(1)}, bf16[32,32,384]{2,1,0:T(8,128)(2,1)S(1)}, u32[]{:S(2)}, u32[]{:S(2)}) %collective-permute-start.1) | collective-permute-done | bytes 786464 | tf_op jit(solution)/shard_map/ppermute | solution.py:12
  27.2 0.0 copy-start
  27.2 1.5 %add_add_fusion = f32[1024,384]{1,0:T(8,128)S(1)} fusion(f32[1024,384]{1,0:T(8,128)S(1)} %fusion.8, f32[1024,384]{1,0:T(8,128)S(1)} %fusion.10, bf16[1152,384]{1,0:T(8,128)(2,1)S(1)} %bitcast.18, bf16[1024,384]{1,0:T(8,128)(2,1)S(1)} %bitcast.24, bf16[1024,384]{1,0:T(8,128)(2,1)S(1)} %bitcast.21, bf16[1024,384]{1,0:T(8,128)(2,1)S(1)} %bitcast.23), kind=kOutput, calls=%fused_computation.7 | convolution fusion | flops 913833984 | bytes 7962624 | tf_op jit(solution)/shard_map/dot_general | solution.py:21
  28.7 0.0 copy-done
  28.7 1.2 %add_convert_fusion = bf16[32,32,384]{2,1,0:T(8,128)(2,1)} fusion(f32[32,32,384]{2,1,0:T(8,128)S(1)} %bitcast.17, bf16[32,32,384]{2,1,0:T(8,128)(2,1)S(1)} %copy-done, f32[384]{0:T(512)S(1)} %get-tuple-element.6, f32[384]{0:T(512)S(1)} %get-tuple-element.5), kind=kLoop, calls=%fused_computation.6 | loop fusion | flops 1966080 | bytes 3148800 | tf_op jit(solution)/shard_map/convert_element_type | solution.py:52
  (5 shorter events, 0.1 us)
Async XLA Ops:
  0.0 7.6 %copy-start.2 = (bf16[360,2,384]{2,1,0:T(2,128)(2,1)S(1)}, bf16[360,2,384]{2,1,0:T(2,128)(2,1)}, u32[]{:S(2)}) copy-start(bf16[360,2,384]{2,1,0:T(2,128)(2,1)} %param.6) | copy-start | bytes 1658884
  0.0 8.6 %copy-start.1 = (bf16[3,3,384,384]{3,2,1,0:T(8,128)(2,1)S(1)}, bf16[3,3,384,384]{3,2,1,0:T(8,128)(2,1)}, u32[]{:S(2)}) copy-start(bf16[3,3,384,384]{3,2,1,0:T(8,128)(2,1)} %param.5) | copy-start | bytes 7962628
  1.4 21.7 %collective-permute-start = (bf16[32,32,384]{2,1,0:T(8,128)(2,1)S(1)}, bf16[32,32,384]{2,1,0:T(8,128)(2,1)S(1)}, u32[]{:S(2)}, u32[]{:S(2)}) collective-permute-start(bf16[32,32,384]{2,1,0:T(8,128)(2,1)S(1)} %broadcast_maximum_fusion), channel_id=1, source_target_pairs={{0,16},{4,20},{8,24},{12,28},{1,17},{5,21},{9,25},{13,29},{2,18},{... | collective-permute-start | bytes 2359304 | tf_op jit(solution)/shard_map/ppermute | solution.py:12
  6.3 20.9 %collective-permute-start.1 = (bf16[32,32,384]{2,1,0:T(8,128)(2,1)S(1)}, bf16[32,32,384]{2,1,0:T(8,128)(2,1)S(1)}, u32[]{:S(2)}, u32[]{:S(2)}) collective-permute-start(bf16[32,32,384]{2,1,0:T(8,128)(2,1)S(1)} %broadcast_maximum_fusion), channel_id=1, source_target_pairs={{16,0},{20,4},{24,8},{28,12},{17,1},{21,5},{25,9},{29,13},{18,2},{... | collective-permute-start | bytes 2359304 | tf_op jit(solution)/shard_map/ppermute | solution.py:12
  27.2 1.5 %copy-start = (bf16[32,32,384]{2,1,0:T(8,128)(2,1)S(1)}, bf16[32,32,384]{2,1,0:T(8,128)(2,1)}, u32[]{:S(2)}) copy-start(bf16[32,32,384]{2,1,0:T(8,128)(2,1)} %param.4) | copy-start | bytes 2359300
where the time goes:
time: 30 us; the launch traced here: 29.8 us
  waiting for transfers between devices  15.4 us (51%)
  starting transfers between devices  6.21 us (21%)
  matrix products  4.51 us (15%)
  other arithmetic  2.56 us (9%)
  between operations  0.76 us (3%)
  local copies, waits for them, and re-layouts  0.39 us (1%)
    ppermute x2, waiting for transfers between devices, shifted(): return lax.ppermute(block, axis, route)  15.4 us
    ppermute x2, starting transfers between devices, shifted(): return lax.ppermute(block, axis, route)  6.21 us
    dot_general x3, matrix products, tap_product(): jnp.dot(flat, filter_kernel.reshape(count * chans, filter_kernel.shape[-1...  4.34 us
    max x1, other arithmetic, local(): active = jnp.maximum(encoded, jnp.zeros((), jnp.bfloat16))  1.36 us
    convert_element_type x1, other arithmetic, local(): return updated.astype(jnp.bfloat16)  1.16 us
  transfers between devices with their start and end apart: 2, of which 2 were waited for; matrix products, arithmetic and copies ran while one was open for 12% of the time, Pallas kernels for 0%

commit v1 on v0

v1 whole, which is shorter than its diff:
```python
import functools

import jax
import jax.numpy as jnp
from jax import lax
from jax.experimental import pallas as pl
from jax.experimental.pallas import tpu as pltpu
from jax.sharding import PartitionSpec as P

DILATION_RATE = 128
MIB = 1 << 20


def shifted(block, axis, distance):
    devices = range(lax.axis_size(axis))
    route = [(i - distance, i) for i in devices if i - distance in devices]
    return lax.ppermute(block, axis, route)


def relu(block):
    return jnp.maximum(block, jnp.zeros((), block.dtype))


def product(block, tap):
    flat = relu(block).reshape(-1, block.shape[-1])
    return jnp.dot(flat, tap, preferred_element_type=jnp.float32)


def film(film_table, lead):
    chosen = lax.dynamic_index_in_dim(film_table, lead[0], 0, keepdims=False)
    chosen = chosen.astype(jnp.float32)
    return 1.0 + chosen[0], chosen[1]


def any_grid(encoded, conv_weight, film_table, lead, row_step, column_step):
    steps = (-1, 0, 1)
    total = jnp.zeros((encoded.shape[0] * encoded.shape[1], encoded.shape[2]), jnp.float32)
    for ky in steps:
        if abs(ky) * row_step >= lax.axis_size("rows"):
            continue
        strip = shifted(encoded, "rows", -ky * row_step) if ky else encoded
        for kx in steps:
            if abs(kx) * column_step >= lax.axis_size("cols"):
                continue
            block = shifted(strip, "cols", -kx * column_step) if kx else strip
            total = total + product(block, conv_weight[ky + 1, kx + 1])
    scale, beta = film(film_table, lead)
    flat = encoded.reshape(total.shape).astype(jnp.float32)
    return (flat + total * scale + beta).astype(jnp.bfloat16).reshape(encoded.shape)


def finish_kernel(step, other_ref, tap_ref, base_ref, scale_ref, out_ref, stage, sems):
    copies = []
    for k in range(base_ref.shape[0] // step):
        rows = pl.ds(k * step, step)
        active = jnp.maximum(other_ref[rows, :], jnp.zeros((), jnp.bfloat16))
        part = jnp.dot(active, tap_ref[...], preferred_element_type=jnp.float32)
        stage[rows, :] = (base_ref[rows, :] + part * scale_ref[...]).astype(jnp.bfloat16)
        copy = pltpu.make_async_copy(stage.at[rows, :], out_ref.at[rows, :], sems.at[k])
        copy.start()
        copies.append(copy)
    for copy in copies:
        copy.wait()


def finish(other, tap, base, scale):
    cells, chans = base.shape
    step = cells // 4
    whole = pl.BlockSpec(memory_space=pltpu.VMEM)
    return pl.pallas_call(
        functools.partial(finish_kernel, step),
        out_shape=jax.ShapeDtypeStruct(base.shape, jnp.bfloat16),
        in_specs=[whole] * 4,
        out_specs=pl.BlockSpec(memory_space=pl.ANY),
        scratch_shapes=[
            pltpu.VMEM((cells, chans), jnp.bfloat16),
            pltpu.SemaphoreType.DMA((cells // step,)),
        ],
        compiler_params=pltpu.CompilerParams(vmem_limit_bytes=16 * MIB),
        cost_estimate=pl.CostEstimate(
            flops=2 * cells * chans * chans,
            bytes_accessed=10 * cells * chans,
            transcendentals=0,
        ),
    )(other, tap, base, scale)


def paired(encoded, conv_weight, film_table, lead, row_step):
    count = lax.axis_size("rows")
    other = lax.ppermute(encoded, "rows", [(i, (i + row_step) % count) for i in range(count)])
    above = lax.axis_index("rows") < row_step
    column = conv_weight[:, 1]
    far_tap = lax.dynamic_index_in_dim(column, jnp.where(above, 2, 0), 0, keepdims=False)
    scale, beta = film(film_table, lead)
    near = product(encoded, column[1])
    base = encoded.reshape(near.shape).astype(jnp.float32) + near * scale + beta
    updated = finish(other.reshape(near.shape), far_tap, base, scale[None])
    return updated.reshape(encoded.shape)


def local(encoded, conv_weight, film_table, lead):
    row_step = DILATION_RATE // encoded.shape[0]
    column_step = DILATION_RATE // encoded.shape[1]
    if lax.axis_size("rows") == 2 * row_step and column_step >= lax.axis_size("cols"):
        return paired(encoded, conv_weight, film_table, lead, row_step)
    return any_grid(encoded, conv_weight, film_table, lead, row_step, column_step)


def solution(mesh):
    placed = (P("rows", "cols", None), P(), P(), P())
    return jax.shard_map(
        local, mesh=mesh, in_specs=placed, out_specs=P("rows", "cols", None), check_vma=False
    )
```

time: 30 us -> 22.3 us (0.74)
  starting transfers between devices: 6.21 us -> 2.97 us
  matrix products: 4.51 us -> 1.62 us
  other arithmetic: 2.56 us -> 0.78 us
  Pallas kernels: 0 us -> 1.35 us
  waiting for transfers between devices: 15.4 us -> 14.7 us
  local copies, waits for them, and re-layouts: 0.39 us -> 0.05 us
    ppermute x2 -> x1, starting transfers between devices: 6.21 us -> 2.97 us  [paired(): lax.ppermute(encoded, 'rows', [(i, (i + row_step) % count) for i in range...]
    dot_general x4 -> x1, matrix products: 4.51 us -> 1.62 us  [product(): return jnp.dot(flat, tap, preferred_element_type=jnp.float32)]
    pallas_call x0 -> x1, Pallas kernels: none -> 1.35 us  [finish(): pl.pallas_call(functools.partial(finish_kernel, step), out_shape=jax.Shap...]
    max x1, other arithmetic: 1.36 us -> 0.07 us  [relu(): return jnp.maximum(block, jnp.zeros((), block.dtype))]
    ppermute x2 -> x1, waiting for transfers between devices: 15.4 us -> 14.7 us  [paired(): lax.ppermute(encoded, 'rows', [(i, (i + row_step) % count) for i in range...]
    convert_element_type x1, other arithmetic: 1.16 us -> 0.69 us  [film(): chosen = chosen.astype(jnp.float32)]
  transfers between devices with their start and end apart: 2 -> 1, of which waited for: 2 -> 1; matrix products, arithmetic and copies ran while one was open for 12% -> 11% of each run, Pallas kernels for 0% -> 0%
where the time goes in v1:
time: 22.3 us; the launch traced here: 22.1 us
  waiting for transfers between devices  14.7 us (66%)
  starting transfers between devices  2.97 us (13%)
  matrix products  1.62 us (7%)
  Pallas kernels  1.35 us (6%)
  other arithmetic  0.78 us (3%)
  between operations  0.7 us (3%)
    ppermute x1, waiting for transfers between devices, paired(): lax.ppermute(encoded, 'rows', [(i, (i + row_step) % count) for i in range...  14.7 us
    ppermute x1, starting transfers between devices, paired(): lax.ppermute(encoded, 'rows', [(i, (i + row_step) % count) for i in range...  2.97 us
    dot_general x1, matrix products, product(): return jnp.dot(flat, tap, preferred_element_type=jnp.float32)  1.62 us
    pallas_call x1, Pallas kernels, finish(): pl.pallas_call(functools.partial(finish_kernel, step), out_shape=jax.Shap...  1.35 us
    convert_element_type x1, other arithmetic, film(): chosen = chosen.astype(jnp.float32)  0.69 us
  transfers between devices with their start and end apart: 1, of which 1 were waited for; matrix products, arithmetic and copies ran while one was open for 11% of the time, Pallas kernels for 0%

profile of v1, /device:TPU:0, one launch (start us, length us, event | category | flops | bytes accessed | tf_op | source)
XLA Modules:
  0.0 22.1 jit_solution(13383616454258235473)
XLA Ops:
  0.0 0.0 copy-start
  0.0 0.0 slice-start
  0.0 3.0 %collective-permute-start = (bf16[32,32,384]{2,1,0:T(8,128)(2,1)}, bf16[32,32,384]{2,1,0:T(8,128)(2,1)S(1)}, u32[]{:S(2)}, u32[]{:S(2)}) collective-permute-start(bf16[32,32,384]{2,1,0:T(8,128)(2,1)} %param.4), channel_id=1, source_target_pairs={{0,16},{4,20},{8,24},{12,28},{16,0},{20,4},{24,8},{28,12},{1,17},{... | collective-permute-start | bytes 2359304 | tf_op jit(solution)/shard_map/ppermute | solution.py:90
  3.6 0.7 %dynamic-slice_convert_fusion = f32[1,2,384]{2,1,0:T(2,128)S(1)} fusion(bf16[360,2,384]{2,1,0:T(2,128)(2,1)} %param.6, s32[]{:T(128)S(6)} %select_n.11), kind=kLoop, calls=%fused_computation.8 | loop fusion | flops 768 | bytes 4612 | tf_op jit(solution)/shard_map/convert_element_type | solution.py:31
  4.3 0.0 slice-done
  4.4 0.0 copy-done
  4.4 0.1 broadcast_maximum_fusion
  4.5 1.6 %fusion.base_ref = f32[1024,384]{1,0:T(8,128)S(1)} fusion(bf16[1024,384]{1,0:T(8,128)(2,1)S(1)} %bitcast.18, bf16[1024,384]{1,0:T(8,128)(2,1)S(1)} %bitcast.19, f32[384]{0:T(512)S(1)} %get-tuple-element.6, f32[384]{0:T(512)S(1)} %get-tuple-element.5, bf16[3,3,384,384]{3,2,1,0:T(8,128)(2,1)} %param.5), kind=kOutput, calls=%fused_computation.1 | convolution fusion | flops 303562752 | bytes 3443712 | tf_op jit(solution)/shard_map/dot_general | solution.py:26
  6.1 14.7 %collective-permute-done = bf16[32,32,384]{2,1,0:T(8,128)(2,1)S(1)} collective-permute-done((bf16[32,32,384]{2,1,0:T(8,128)(2,1)}, bf16[32,32,384]{2,1,0:T(8,128)(2,1)S(1)}, u32[]{:S(2)}, u32[]{:S(2)}) %collective-permute-start) | collective-permute-done | bytes 786464 | tf_op jit(solution)/shard_map/ppermute | solution.py:90
  20.8 1.3 %shard_map.46 = bf16[1024,384]{1,0:T(8,128)(2,1)} custom-call(bf16[1024,384]{1,0:T(8,128)(2,1)S(1)} %bitcast.17, bf16[384,384]{1,0:T(8,128)(2,1)S(1)} %dynamic-slice_bitcast_fusion.tap_ref, f32[1024,384]{1,0:T(8,128)S(1)} %fusion.base_ref, f32[1,384]{1,0:T(1,128)S(1)} %get-tuple-element.7.scale_ref), custom_call_target="tpu_custom_call" | custom-call | flops 301989888 | bytes 3932160 | tf_op jit(solution)/shard_map/pallas_call | solution.py:70
  (2 shorter events, 0.1 us)
Async XLA Ops:
  0.0 4.4 %copy-start = (bf16[32,32,384]{2,1,0:T(8,128)(2,1)S(1)}, bf16[32,32,384]{2,1,0:T(8,128)(2,1)}, u32[]{:S(2)}) copy-start(bf16[32,32,384]{2,1,0:T(8,128)(2,1)} %param.4) | copy-start | bytes 2359300
  0.0 4.3 %slice-start = ((bf16[3,3,384,384]{3,2,1,0:T(8,128)(2,1)}), bf16[3,1,384,384]{3,2,1,0:T(8,128)(2,1)S(1)}, s32[]{:S(2)}) async-start(bf16[3,3,384,384]{3,2,1,0:T(8,128)(2,1)} %param.5), calls=%async_computation | async-start | bytes 1769472 | tf_op jit(solution)/shard_map/slice | solution.py:92
  0.0 20.8 %collective-permute-start = (bf16[32,32,384]{2,1,0:T(8,128)(2,1)}, bf16[32,32,384]{2,1,0:T(8,128)(2,1)S(1)}, u32[]{:S(2)}, u32[]{:S(2)}) collective-permute-start(bf16[32,32,384]{2,1,0:T(8,128)(2,1)} %param.4), channel_id=1, source_target_pairs={{0,16},{4,20},{8,24},{12,28},{16,0},{20,4},{24,8},{28,12},{1,17},{... | collective-permute-start | bytes 2359304 | tf_op jit(solution)/shard_map/ppermute | solution.py:90

commit v2 on v1

--- a/solution.py
+++ b/solution.py
@@ -49,10 +49,10 @@
     return (flat + total * scale + beta).astype(jnp.bfloat16).reshape(encoded.shape)
 
 
-def finish_kernel(step, other_ref, tap_ref, base_ref, scale_ref, out_ref, stage, sems):
+def finish_kernel(cuts, other_ref, tap_ref, base_ref, scale_ref, out_ref, stage, sems):
     copies = []
-    for k in range(base_ref.shape[0] // step):
-        rows = pl.ds(k * step, step)
+    for k, (start, stop) in enumerate(zip(cuts[:-1], cuts[1:])):
+        rows = pl.ds(start, stop - start)
         active = jnp.maximum(other_ref[rows, :], jnp.zeros((), jnp.bfloat16))
         part = jnp.dot(active, tap_ref[...], preferred_element_type=jnp.float32)
         stage[rows, :] = (base_ref[rows, :] + part * scale_ref[...]).astype(jnp.bfloat16)
@@ -65,16 +65,16 @@
 
 def finish(other, tap, base, scale):
     cells, chans = base.shape
-    step = cells // 4
+    cuts = [cells * eighth // 8 for eighth in (0, 2, 4, 6, 7, 8)]
     whole = pl.BlockSpec(memory_space=pltpu.VMEM)
     return pl.pallas_call(
-        functools.partial(finish_kernel, step),
+        functools.partial(finish_kernel, cuts),
         out_shape=jax.ShapeDtypeStruct(base.shape, jnp.bfloat16),
         in_specs=[whole] * 4,
         out_specs=pl.BlockSpec(memory_space=pl.ANY),
         scratch_shapes=[
             pltpu.VMEM((cells, chans), jnp.bfloat16),
-            pltpu.SemaphoreType.DMA((cells // step,)),
+            pltpu.SemaphoreType.DMA((len(cuts) - 1,)),
         ],
         compiler_params=pltpu.CompilerParams(vmem_limit_bytes=16 * MIB),
         cost_estimate=pl.CostEstimate(

time: 22.3 us -> 22.3 us (level)
  no operation moved by 1% of the time
where the time goes in v2:
time: 22.3 us; the launch traced here: 22.1 us
  waiting for transfers between devices  14.7 us (66%)
  starting transfers between devices  2.97 us (13%)
  matrix products  1.62 us (7%)
  Pallas kernels  1.32 us (6%)
  other arithmetic  0.78 us (3%)
  between operations  0.7 us (3%)
    ppermute x1, waiting for transfers between devices, paired(): lax.ppermute(encoded, 'rows', [(i, (i + row_step) % count) for i in range...  14.7 us
    ppermute x1, starting transfers between devices, paired(): lax.ppermute(encoded, 'rows', [(i, (i + row_step) % count) for i in range...  2.97 us
    dot_general x1, matrix products, product(): return jnp.dot(flat, tap, preferred_element_type=jnp.float32)  1.62 us
    pallas_call x1, Pallas kernels, finish(): pl.pallas_call(functools.partial(finish_kernel, cuts), out_shape=jax.Shap...  1.32 us
    convert_element_type x1, other arithmetic, film(): chosen = chosen.astype(jnp.float32)  0.69 us
  transfers between devices with their start and end apart: 1, of which 1 were waited for; matrix products, arithmetic and copies ran while one was open for 11% of the time, Pallas kernels for 0%

profile of v2, /device:TPU:0, one launch (start us, length us, event | category | flops | bytes accessed | tf_op | source)
XLA Modules:
  0.0 22.1 jit_solution(4514819074131169984)
XLA Ops:
  0.0 0.0 copy-start
  0.0 0.0 slice-start
  0.0 3.0 %collective-permute-start = (bf16[32,32,384]{2,1,0:T(8,128)(2,1)}, bf16[32,32,384]{2,1,0:T(8,128)(2,1)S(1)}, u32[]{:S(2)}, u32[]{:S(2)}) collective-permute-start(bf16[32,32,384]{2,1,0:T(8,128)(2,1)} %param.4), channel_id=1, source_target_pairs={{0,16},{4,20},{8,24},{12,28},{16,0},{20,4},{24,8},{28,12},{1,17},{... | collective-permute-start | bytes 2359304 | tf_op jit(solution)/shard_map/ppermute | solution.py:90
  3.6 0.7 %dynamic-slice_convert_fusion = f32[1,2,384]{2,1,0:T(2,128)S(1)} fusion(bf16[360,2,384]{2,1,0:T(2,128)(2,1)} %param.6, s32[]{:T(128)S(6)} %select_n.11), kind=kLoop, calls=%fused_computation.8 | loop fusion | flops 768 | bytes 4612 | tf_op jit(solution)/shard_map/convert_element_type | solution.py:31
  4.3 0.0 slice-done
  4.4 0.0 copy-done
  4.4 0.1 broadcast_maximum_fusion
  4.5 1.6 %fusion.base_ref = f32[1024,384]{1,0:T(8,128)S(1)} fusion(bf16[1024,384]{1,0:T(8,128)(2,1)S(1)} %bitcast.18, bf16[1024,384]{1,0:T(8,128)(2,1)S(1)} %bitcast.19, f32[384]{0:T(512)S(1)} %get-tuple-element.6, f32[384]{0:T(512)S(1)} %get-tuple-element.5, bf16[3,3,384,384]{3,2,1,0:T(8,128)(2,1)} %param.5), kind=kOutput, calls=%fused_computation.1 | convolution fusion | flops 303562752 | bytes 3443712 | tf_op jit(solution)/shard_map/dot_general | solution.py:26
  6.1 14.7 %collective-permute-done = bf16[32,32,384]{2,1,0:T(8,128)(2,1)S(1)} collective-permute-done((bf16[32,32,384]{2,1,0:T(8,128)(2,1)}, bf16[32,32,384]{2,1,0:T(8,128)(2,1)S(1)}, u32[]{:S(2)}, u32[]{:S(2)}) %collective-permute-start) | collective-permute-done | bytes 786464 | tf_op jit(solution)/shard_map/ppermute | solution.py:90
  20.8 1.3 %shard_map.46 = bf16[1024,384]{1,0:T(8,128)(2,1)} custom-call(bf16[1024,384]{1,0:T(8,128)(2,1)S(1)} %bitcast.17, bf16[384,384]{1,0:T(8,128)(2,1)S(1)} %dynamic-slice_bitcast_fusion.tap_ref, f32[1024,384]{1,0:T(8,128)S(1)} %fusion.base_ref, f32[1,384]{1,0:T(1,128)S(1)} %get-tuple-element.7.scale_ref), custom_call_target="tpu_custom_call" | custom-call | flops 301989888 | bytes 3932160 | tf_op jit(solution)/shard_map/pallas_call | solution.py:70
  (2 shorter events, 0.1 us)
Async XLA Ops:
  0.0 4.4 %copy-start = (bf16[32,32,384]{2,1,0:T(8,128)(2,1)S(1)}, bf16[32,32,384]{2,1,0:T(8,128)(2,1)}, u32[]{:S(2)}) copy-start(bf16[32,32,384]{2,1,0:T(8,128)(2,1)} %param.4) | copy-start | bytes 2359300
  0.0 4.3 %slice-start = ((bf16[3,3,384,384]{3,2,1,0:T(8,128)(2,1)}), bf16[3,1,384,384]{3,2,1,0:T(8,128)(2,1)S(1)}, s32[]{:S(2)}) async-start(bf16[3,3,384,384]{3,2,1,0:T(8,128)(2,1)} %param.5), calls=%async_computation | async-start | bytes 1769472 | tf_op jit(solution)/shard_map/slice | solution.py:92
  0.0 20.8 %collective-permute-start = (bf16[32,32,384]{2,1,0:T(8,128)(2,1)}, bf16[32,32,384]{2,1,0:T(8,128)(2,1)S(1)}, u32[]{:S(2)}, u32[]{:S(2)}) collective-permute-start(bf16[32,32,384]{2,1,0:T(8,128)(2,1)} %param.4), channel_id=1, source_target_pairs={{0,16},{4,20},{8,24},{12,28},{16,0},{20,4},{24,8},{28,12},{1,17},{... | collective-permute-start | bytes 2359304 | tf_op jit(solution)/shard_map/ppermute | solution.py:90

commit v3 on v2

--- a/solution.py
+++ b/solution.py
@@ -65,7 +65,7 @@
 
 def finish(other, tap, base, scale):
     cells, chans = base.shape
-    cuts = [cells * eighth // 8 for eighth in (0, 2, 4, 6, 7, 8)]
+    cuts = [cells * eighth // 8 for eighth in (0, 1, 2, 4, 6, 7, 8)]
     whole = pl.BlockSpec(memory_space=pltpu.VMEM)
     return pl.pallas_call(
         functools.partial(finish_kernel, cuts),

time: 22.3 us -> 22.3 us (level)
  no operation moved by 1% of the time
where the time goes in v3:
time: 22.3 us; the launch traced here: 22.1 us
  waiting for transfers between devices  14.7 us (66%)
  starting transfers between devices  2.97 us (13%)
  matrix products  1.62 us (7%)
  Pallas kernels  1.34 us (6%)
  other arithmetic  0.78 us (3%)
  between operations  0.7 us (3%)
    ppermute x1, waiting for transfers between devices, paired(): lax.ppermute(encoded, 'rows', [(i, (i + row_step) % count) for i in range...  14.7 us
    ppermute x1, starting transfers between devices, paired(): lax.ppermute(encoded, 'rows', [(i, (i + row_step) % count) for i in range...  2.97 us
    dot_general x1, matrix products, product(): return jnp.dot(flat, tap, preferred_element_type=jnp.float32)  1.62 us
    pallas_call x1, Pallas kernels, finish(): pl.pallas_call(functools.partial(finish_kernel, cuts), out_shape=jax.Shap...  1.34 us
    convert_element_type x1, other arithmetic, film(): chosen = chosen.astype(jnp.float32)  0.69 us
  transfers between devices with their start and end apart: 1, of which 1 were waited for; matrix products, arithmetic and copies ran while one was open for 11% of the time, Pallas kernels for 0%

profile of v3, /device:TPU:0, one launch (start us, length us, event | category | flops | bytes accessed | tf_op | source)
XLA Modules:
  0.0 22.1 jit_solution(7787039672882109750)
XLA Ops:
  0.0 0.0 copy-start
  0.0 0.0 slice-start
  0.0 3.0 %collective-permute-start = (bf16[32,32,384]{2,1,0:T(8,128)(2,1)}, bf16[32,32,384]{2,1,0:T(8,128)(2,1)S(1)}, u32[]{:S(2)}, u32[]{:S(2)}) collective-permute-start(bf16[32,32,384]{2,1,0:T(8,128)(2,1)} %param.4), channel_id=1, source_target_pairs={{0,16},{4,20},{8,24},{12,28},{16,0},{20,4},{24,8},{28,12},{1,17},{... | collective-permute-start | bytes 2359304 | tf_op jit(solution)/shard_map/ppermute | solution.py:90
  3.6 0.7 %dynamic-slice_convert_fusion = f32[1,2,384]{2,1,0:T(2,128)S(1)} fusion(bf16[360,2,384]{2,1,0:T(2,128)(2,1)} %param.6, s32[]{:T(128)S(6)} %select_n.11), kind=kLoop, calls=%fused_computation.8 | loop fusion | flops 768 | bytes 4612 | tf_op jit(solution)/shard_map/convert_element_type | solution.py:31
  4.3 0.0 slice-done
  4.4 0.0 copy-done
  4.4 0.1 broadcast_maximum_fusion
  4.5 1.6 %fusion.base_ref = f32[1024,384]{1,0:T(8,128)S(1)} fusion(bf16[1024,384]{1,0:T(8,128)(2,1)S(1)} %bitcast.18, bf16[1024,384]{1,0:T(8,128)(2,1)S(1)} %bitcast.19, f32[384]{0:T(512)S(1)} %get-tuple-element.6, f32[384]{0:T(512)S(1)} %get-tuple-element.5, bf16[3,3,384,384]{3,2,1,0:T(8,128)(2,1)} %param.5), kind=kOutput, calls=%fused_computation.1 | convolution fusion | flops 303562752 | bytes 3443712 | tf_op jit(solution)/shard_map/dot_general | solution.py:26
  6.1 14.7 %collective-permute-done = bf16[32,32,384]{2,1,0:T(8,128)(2,1)S(1)} collective-permute-done((bf16[32,32,384]{2,1,0:T(8,128)(2,1)}, bf16[32,32,384]{2,1,0:T(8,128)(2,1)S(1)}, u32[]{:S(2)}, u32[]{:S(2)}) %collective-permute-start) | collective-permute-done | bytes 786464 | tf_op jit(solution)/shard_map/ppermute | solution.py:90
  20.8 1.3 %shard_map.46 = bf16[1024,384]{1,0:T(8,128)(2,1)} custom-call(bf16[1024,384]{1,0:T(8,128)(2,1)S(1)} %bitcast.17, bf16[384,384]{1,0:T(8,128)(2,1)S(1)} %dynamic-slice_bitcast_fusion.tap_ref, f32[1024,384]{1,0:T(8,128)S(1)} %fusion.base_ref, f32[1,384]{1,0:T(1,128)S(1)} %get-tuple-element.7.scale_ref), custom_call_target="tpu_custom_call" | custom-call | flops 301989888 | bytes 3932160 | tf_op jit(solution)/shard_map/pallas_call | solution.py:70
  (2 shorter events, 0.1 us)
Async XLA Ops:
  0.0 4.4 %copy-start = (bf16[32,32,384]{2,1,0:T(8,128)(2,1)S(1)}, bf16[32,32,384]{2,1,0:T(8,128)(2,1)}, u32[]{:S(2)}) copy-start(bf16[32,32,384]{2,1,0:T(8,128)(2,1)} %param.4) | copy-start | bytes 2359300
  0.0 4.3 %slice-start = ((bf16[3,3,384,384]{3,2,1,0:T(8,128)(2,1)}), bf16[3,1,384,384]{3,2,1,0:T(8,128)(2,1)S(1)}, s32[]{:S(2)}) async-start(bf16[3,3,384,384]{3,2,1,0:T(8,128)(2,1)} %param.5), calls=%async_computation | async-start | bytes 1769472 | tf_op jit(solution)/shard_map/slice | solution.py:92
  0.0 20.8 %collective-permute-start = (bf16[32,32,384]{2,1,0:T(8,128)(2,1)}, bf16[32,32,384]{2,1,0:T(8,128)(2,1)S(1)}, u32[]{:S(2)}, u32[]{:S(2)}) collective-permute-start(bf16[32,32,384]{2,1,0:T(8,128)(2,1)} %param.4), channel_id=1, source_target_pairs={{0,16},{4,20},{8,24},{12,28},{16,0},{20,4},{24,8},{28,12},{1,17},{... | collective-permute-start | bytes 2359304 | tf_op jit(solution)/shard_map/ppermute | solution.py:90

commit v4 on v3

--- a/solution.py
+++ b/solution.py
@@ -65,7 +65,7 @@
 
 def finish(other, tap, base, scale):
     cells, chans = base.shape
-    cuts = [cells * eighth // 8 for eighth in (0, 1, 2, 4, 6, 7, 8)]
+    cuts = [cells * eighth // 8 for eighth in (0, 4, 6, 7, 8)]
     whole = pl.BlockSpec(memory_space=pltpu.VMEM)
     return pl.pallas_call(
         functools.partial(finish_kernel, cuts),

time: 22.3 us -> 22.3 us (level)
  no operation moved by 1% of the time
where the time goes in v4:
time: 22.3 us; the launch traced here: 22.1 us
  waiting for transfers between devices  14.7 us (66%)
  starting transfers between devices  2.97 us (13%)
  matrix products  1.62 us (7%)
  Pallas kernels  1.34 us (6%)
  other arithmetic  0.78 us (3%)
  between operations  0.7 us (3%)
    ppermute x1, waiting for transfers between devices, paired(): lax.ppermute(encoded, 'rows', [(i, (i + row_step) % count) for i in range...  14.7 us
    ppermute x1, starting transfers between devices, paired(): lax.ppermute(encoded, 'rows', [(i, (i + row_step) % count) for i in range...  2.97 us
    dot_general x1, matrix products, product(): return jnp.dot(flat, tap, preferred_element_type=jnp.float32)  1.62 us
    pallas_call x1, Pallas kernels, finish(): pl.pallas_call(functools.partial(finish_kernel, cuts), out_shape=jax.Shap...  1.34 us
    convert_element_type x1, other arithmetic, film(): chosen = chosen.astype(jnp.float32)  0.69 us
  transfers between devices with their start and end apart: 1, of which 1 were waited for; matrix products, arithmetic and copies ran while one was open for 11% of the time, Pallas kernels for 0%

profile of v4, /device:TPU:0, one launch (start us, length us, event | category | flops | bytes accessed | tf_op | source)
XLA Modules:
  0.0 22.1 jit_solution(11132574249995592590)
XLA Ops:
  0.0 0.0 copy-start
  0.0 0.0 slice-start
  0.0 3.0 %collective-permute-start = (bf16[32,32,384]{2,1,0:T(8,128)(2,1)}, bf16[32,32,384]{2,1,0:T(8,128)(2,1)S(1)}, u32[]{:S(2)}, u32[]{:S(2)}) collective-permute-start(bf16[32,32,384]{2,1,0:T(8,128)(2,1)} %param.4), channel_id=1, source_target_pairs={{0,16},{4,20},{8,24},{12,28},{16,0},{20,4},{24,8},{28,12},{1,17},{... | collective-permute-start | bytes 2359304 | tf_op jit(solution)/shard_map/ppermute | solution.py:90
  3.6 0.7 %dynamic-slice_convert_fusion = f32[1,2,384]{2,1,0:T(2,128)S(1)} fusion(bf16[360,2,384]{2,1,0:T(2,128)(2,1)} %param.6, s32[]{:T(128)S(6)} %select_n.11), kind=kLoop, calls=%fused_computation.8 | loop fusion | flops 768 | bytes 4612 | tf_op jit(solution)/shard_map/convert_element_type | solution.py:31
  4.3 0.0 slice-done
  4.4 0.0 copy-done
  4.4 0.1 broadcast_maximum_fusion
  4.5 1.6 %fusion.base_ref = f32[1024,384]{1,0:T(8,128)S(1)} fusion(bf16[1024,384]{1,0:T(8,128)(2,1)S(1)} %bitcast.18, bf16[1024,384]{1,0:T(8,128)(2,1)S(1)} %bitcast.19, f32[384]{0:T(512)S(1)} %get-tuple-element.6, f32[384]{0:T(512)S(1)} %get-tuple-element.5, bf16[3,3,384,384]{3,2,1,0:T(8,128)(2,1)} %param.5), kind=kOutput, calls=%fused_computation.1 | convolution fusion | flops 303562752 | bytes 3443712 | tf_op jit(solution)/shard_map/dot_general | solution.py:26
  6.1 14.7 %collective-permute-done = bf16[32,32,384]{2,1,0:T(8,128)(2,1)S(1)} collective-permute-done((bf16[32,32,384]{2,1,0:T(8,128)(2,1)}, bf16[32,32,384]{2,1,0:T(8,128)(2,1)S(1)}, u32[]{:S(2)}, u32[]{:S(2)}) %collective-permute-start) | collective-permute-done | bytes 786464 | tf_op jit(solution)/shard_map/ppermute | solution.py:90
  20.8 1.3 %shard_map.46 = bf16[1024,384]{1,0:T(8,128)(2,1)} custom-call(bf16[1024,384]{1,0:T(8,128)(2,1)S(1)} %bitcast.17, bf16[384,384]{1,0:T(8,128)(2,1)S(1)} %dynamic-slice_bitcast_fusion.tap_ref, f32[1024,384]{1,0:T(8,128)S(1)} %fusion.base_ref, f32[1,384]{1,0:T(1,128)S(1)} %get-tuple-element.7.scale_ref), custom_call_target="tpu_custom_call" | custom-call | flops 301989888 | bytes 3932160 | tf_op jit(solution)/shard_map/pallas_call | solution.py:70
  (2 shorter events, 0.1 us)
Async XLA Ops:
  0.0 4.4 %copy-start = (bf16[32,32,384]{2,1,0:T(8,128)(2,1)S(1)}, bf16[32,32,384]{2,1,0:T(8,128)(2,1)}, u32[]{:S(2)}) copy-start(bf16[32,32,384]{2,1,0:T(8,128)(2,1)} %param.4) | copy-start | bytes 2359300
  0.0 4.3 %slice-start = ((bf16[3,3,384,384]{3,2,1,0:T(8,128)(2,1)}), bf16[3,1,384,384]{3,2,1,0:T(8,128)(2,1)S(1)}, s32[]{:S(2)}) async-start(bf16[3,3,384,384]{3,2,1,0:T(8,128)(2,1)} %param.5), calls=%async_computation | async-start | bytes 1769472 | tf_op jit(solution)/shard_map/slice | solution.py:92
  0.0 20.8 %collective-permute-start = (bf16[32,32,384]{2,1,0:T(8,128)(2,1)}, bf16[32,32,384]{2,1,0:T(8,128)(2,1)S(1)}, u32[]{:S(2)}, u32[]{:S(2)}) collective-permute-start(bf16[32,32,384]{2,1,0:T(8,128)(2,1)} %param.4), channel_id=1, source_target_pairs={{0,16},{4,20},{8,24},{12,28},{16,0},{20,4},{24,8},{28,12},{1,17},{... | collective-permute-start | bytes 2359304 | tf_op jit(solution)/shard_map/ppermute | solution.py:90

commit v5 on v4

--- a/solution.py
+++ b/solution.py
@@ -49,12 +49,26 @@
     return (flat + total * scale + beta).astype(jnp.bfloat16).reshape(encoded.shape)
 
 
-def finish_kernel(cuts, other_ref, tap_ref, base_ref, scale_ref, out_ref, stage, sems):
+def finish_kernel(
+    cuts, other_ref, tap_ref, twin_ref, base_ref, scale_ref, out_ref, stage, sems
+):
+    deep = tap_ref.shape[0]
+    wide = other_ref.shape[1] - deep
     copies = []
     for k, (start, stop) in enumerate(zip(cuts[:-1], cuts[1:])):
         rows = pl.ds(start, stop - start)
         active = jnp.maximum(other_ref[rows, :], jnp.zeros((), jnp.bfloat16))
-        part = jnp.dot(active, tap_ref[...], preferred_element_type=jnp.float32)
+        part = jnp.dot(active[:, :deep], tap_ref[...], preferred_element_type=jnp.float32)
+        count = (stop - start) // 2
+        twins = jnp.concatenate([active[:count, deep:], active[count:, deep:]], axis=1)
+        rest = jnp.dot(twins, twin_ref[...], preferred_element_type=jnp.float32)
+        halves = [
+            jnp.concatenate(
+                [rest[:, k : k + wide] for k in range(side * wide, rest.shape[1], 2 * wide)], axis=1
+            )
+            for side in range(2)
+        ]
+        part = part + jnp.concatenate(halves, axis=0)
         stage[rows, :] = (base_ref[rows, :] + part * scale_ref[...]).astype(jnp.bfloat16)
         copy = pltpu.make_async_copy(stage.at[rows, :], out_ref.at[rows, :], sems.at[k])
         copy.start()
@@ -63,14 +77,25 @@
         copy.wait()
 
 
+def twin_tap(tap, wide):
+    parts = []
+    for k in range(0, tap.shape[1], wide):
+        part = tap[:, k : k + wide]
+        empty = jnp.zeros_like(part)
+        parts += [jnp.concatenate([part, empty]), jnp.concatenate([empty, part])]
+    return jnp.concatenate(parts, axis=1)
+
+
 def finish(other, tap, base, scale):
     cells, chans = base.shape
-    cuts = [cells * eighth // 8 for eighth in (0, 4, 6, 7, 8)]
+    deep = chans * 2 // 3
+    tap, twin = tap[:deep], twin_tap(tap[deep:], chans - deep)
+    cuts = [cells * eighth // 8 for eighth in (0, 2, 4, 6, 8)]
     whole = pl.BlockSpec(memory_space=pltpu.VMEM)
     return pl.pallas_call(
         functools.partial(finish_kernel, cuts),
         out_shape=jax.ShapeDtypeStruct(base.shape, jnp.bfloat16),
-        in_specs=[whole] * 4,
+        in_specs=[whole] * 5,
         out_specs=pl.BlockSpec(memory_space=pl.ANY),
         scratch_shapes=[
             pltpu.VMEM((cells, chans), jnp.bfloat16),
@@ -82,7 +107,7 @@
             bytes_accessed=10 * cells * chans,
             transcendentals=0,
         ),
-    )(other, tap, base, scale)
+    )(other, tap, twin, base, scale)
 
 
 def paired(encoded, conv_weight, film_table, lead, row_step):

time: 22.3 us -> 22.3 us (level)
  waiting for transfers between devices: 14.7 us -> 13.1 us
  local copies, waits for them, and re-layouts: 0.05 us -> 1.51 us
    ppermute x1, waiting for transfers between devices: 14.7 us -> 13.1 us  [paired(): lax.ppermute(encoded, 'rows', [(i, (i + row_step) % count) for i in range...]
    slice x2 -> x1, local copies, waits for them, and re-layouts: 0.01 us -> 1.34 us  [paired(): column = conv_weight[:, 1]]
  transfers between devices with their start and end apart: 1 -> 1, of which waited for: 1 -> 1; matrix products, arithmetic and copies ran while one was open for 11% -> 18% of each run, Pallas kernels for 0% -> 0%
where the time goes in v5:
time: 22.3 us; the launch traced here: 22.1 us
  waiting for transfers between devices  13.1 us (59%)
  starting transfers between devices  2.97 us (13%)
  matrix products  1.62 us (7%)
  local copies, waits for them, and re-layouts  1.51 us (7%)
  Pallas kernels  1.42 us (6%)
  other arithmetic  0.78 us (3%)
  between operations  0.77 us (3%)
    ppermute x1, waiting for transfers between devices, paired(): lax.ppermute(encoded, 'rows', [(i, (i + row_step) % count) for i in range...  13.1 us
    ppermute x1, starting transfers between devices, paired(): lax.ppermute(encoded, 'rows', [(i, (i + row_step) % count) for i in range...  2.97 us
    dot_general x1, matrix products, product(): return jnp.dot(flat, tap, preferred_element_type=jnp.float32)  1.62 us
    pallas_call x1, Pallas kernels, finish(): pl.pallas_call(functools.partial(finish_kernel, cuts), out_shape=jax.Shap...  1.42 us
    slice x1, local copies, waits for them, and re-layouts, paired(): column = conv_weight[:, 1]  1.34 us
    convert_element_type x1, other arithmetic, film(): chosen = chosen.astype(jnp.float32)  0.69 us
  transfers between devices with their start and end apart: 1, of which 1 were waited for; matrix products, arithmetic and copies ran while one was open for 18% of the time, Pallas kernels for 0%

profile of v5, /device:TPU:0, one launch (start us, length us, event | category | flops | bytes accessed | tf_op | source)
XLA Modules:
  0.0 22.1 jit_solution(891338980868553370)
XLA Ops:
  0.0 3.0 %collective-permute-start = (bf16[32,32,384]{2,1,0:T(8,128)(2,1)}, bf16[32,32,384]{2,1,0:T(8,128)(2,1)S(1)}, u32[]{:S(2)}, u32[]{:S(2)}) collective-permute-start(bf16[32,32,384]{2,1,0:T(8,128)(2,1)} %param.4), channel_id=1, source_target_pairs={{0,16},{4,20},{8,24},{12,28},{16,0},{20,4},{24,8},{28,12},{1,17},{... | collective-permute-start | bytes 2359304 | tf_op jit(solution)/shard_map/ppermute | solution.py:115
  3.6 0.0 copy-start
  3.6 1.3 %slice.37 = bf16[3,1,384,384]{3,2,1,0:T(8,128)(2,1)S(1)} slice(bf16[3,3,384,384]{3,2,1,0:T(8,128)(2,1)} %param.5), slice={[0:3], [1:2], [0:384], [0:384]} | slice | bytes 1769472 | tf_op jit(solution)/shard_map/slice | solution.py:117
  5.2 0.7 %dynamic-slice_convert_fusion = f32[1,2,384]{2,1,0:T(2,128)S(1)} fusion(bf16[360,2,384]{2,1,0:T(2,128)(2,1)} %param.6, s32[]{:T(128)S(6)} %select_n.11), kind=kLoop, calls=%fused_computation.15 | loop fusion | flops 768 | bytes 4612 | tf_op jit(solution)/shard_map/convert_element_type | solution.py:31
  5.9 0.0 copy-done
  5.9 0.1 broadcast_maximum_fusion
  6.0 1.6 %fusion.base_ref = f32[1024,384]{1,0:T(8,128)S(1)} fusion(bf16[1024,384]{1,0:T(8,128)(2,1)S(1)} %bitcast.20, bf16[1024,384]{1,0:T(8,128)(2,1)S(1)} %bitcast.21, f32[384]{0:T(512)S(1)} %get-tuple-element.6, f32[384]{0:T(512)S(1)} %get-tuple-element.5, bf16[3,3,384,384]{3,2,1,0:T(8,128)(2,1)} %param.5), kind=kOutput, calls=%fused_computation.1 | convolution fusion | flops 303562752 | bytes 3443712 | tf_op jit(solution)/shard_map/dot_general | solution.py:26
  7.7 13.1 %collective-permute-done = bf16[32,32,384]{2,1,0:T(8,128)(2,1)S(1)} collective-permute-done((bf16[32,32,384]{2,1,0:T(8,128)(2,1)}, bf16[32,32,384]{2,1,0:T(8,128)(2,1)S(1)}, u32[]{:S(2)}, u32[]{:S(2)}) %collective-permute-start) | collective-permute-done | bytes 786464 | tf_op jit(solution)/shard_map/ppermute | solution.py:115
  20.7 1.4 %shard_map.46 = bf16[1024,384]{1,0:T(8,128)(2,1)} custom-call(bf16[1024,384]{1,0:T(8,128)(2,1)S(1)} %bitcast.19, bf16[256,384]{1,0:T(8,128)(2,1)S(1)} %dynamic-slice_bitcast_fusion.tap_ref, bf16[256,768]{1,0:T(8,128)(2,1)S(1)} %pad_dynamic-update-slice_fusion.twin_ref, f32[1024,384]{1,0:T(8,128)S(1)} %fusion.base_ref, f32[1,384]{1,0:T(1,128)S(1)} %get-tuple-element.10.scale_ref), custom_call_target="tpu_custom_call" | custom-call | flops 301989888 | bytes 3932160 | tf_op jit(solution)/shard_map/pallas_call | solution.py:95
  (10 shorter events, 0.2 us)
Async XLA Ops:
  0.0 20.7 %collective-permute-start = (bf16[32,32,384]{2,1,0:T(8,128)(2,1)}, bf16[32,32,384]{2,1,0:T(8,128)(2,1)S(1)}, u32[]{:S(2)}, u32[]{:S(2)}) collective-permute-start(bf16[32,32,384]{2,1,0:T(8,128)(2,1)} %param.4), channel_id=1, source_target_pairs={{0,16},{4,20},{8,24},{12,28},{16,0},{20,4},{24,8},{28,12},{1,17},{... | collective-permute-start | bytes 2359304 | tf_op jit(solution)/shard_map/ppermute | solution.py:115
  3.6 2.3 %copy-start = (bf16[32,32,384]{2,1,0:T(8,128)(2,1)S(1)}, bf16[32,32,384]{2,1,0:T(8,128)(2,1)}, u32[]{:S(2)}) copy-start(bf16[32,32,384]{2,1,0:T(8,128)(2,1)} %param.4) | copy-start | bytes 2359300

commit v6 on v4

--- a/solution.py
+++ b/solution.py
@@ -50,22 +50,24 @@
 
 
 def finish_kernel(cuts, other_ref, tap_ref, base_ref, scale_ref, out_ref, stage, sems):
+    spans = list(zip(cuts[:-1], cuts[1:]))
     copies = []
-    for k, (start, stop) in enumerate(zip(cuts[:-1], cuts[1:])):
+    for k, (start, stop) in enumerate(spans):
         rows = pl.ds(start, stop - start)
         active = jnp.maximum(other_ref[rows, :], jnp.zeros((), jnp.bfloat16))
         part = jnp.dot(active, tap_ref[...], preferred_element_type=jnp.float32)
         stage[rows, :] = (base_ref[rows, :] + part * scale_ref[...]).astype(jnp.bfloat16)
-        copy = pltpu.make_async_copy(stage.at[rows, :], out_ref.at[rows, :], sems.at[k])
-        copy.start()
-        copies.append(copy)
+        copies.append(pltpu.make_async_copy(stage.at[rows, :], out_ref.at[rows, :], sems.at[k]))
+        if k:
+            copies[k - 1].start()
+    copies[-1].start()
     for copy in copies:
         copy.wait()
 
 
 def finish(other, tap, base, scale):
     cells, chans = base.shape
-    cuts = [cells * eighth // 8 for eighth in (0, 4, 6, 7, 8)]
+    cuts = [cells * eighth // 8 for eighth in (0, 1, 3, 5, 7, 8)]
     whole = pl.BlockSpec(memory_space=pltpu.VMEM)
     return pl.pallas_call(
         functools.partial(finish_kernel, cuts),

time: 22.3 us -> 22.4 us (level)
  no operation moved by 1% of the time
where the time goes in v6:
time: 22.4 us; the launch traced here: 22.2 us
  waiting for transfers between devices  14.7 us (66%)
  starting transfers between devices  2.97 us (13%)
  matrix products  1.62 us (7%)
  Pallas kernels  1.41 us (6%)
  other arithmetic  0.78 us (3%)
  between operations  0.7 us (3%)
    ppermute x1, waiting for transfers between devices, paired(): lax.ppermute(encoded, 'rows', [(i, (i + row_step) % count) for i in range...  14.7 us
    ppermute x1, starting transfers between devices, paired(): lax.ppermute(encoded, 'rows', [(i, (i + row_step) % count) for i in range...  2.97 us
    dot_general x1, matrix products, product(): return jnp.dot(flat, tap, preferred_element_type=jnp.float32)  1.62 us
    pallas_call x1, Pallas kernels, finish(): pl.pallas_call(functools.partial(finish_kernel, cuts), out_shape=jax.Shap...  1.41 us
    convert_element_type x1, other arithmetic, film(): chosen = chosen.astype(jnp.float32)  0.69 us
  transfers between devices with their start and end apart: 1, of which 1 were waited for; matrix products, arithmetic and copies ran while one was open for 11% of the time, Pallas kernels for 0%

profile of v6, /device:TPU:0, one launch (start us, length us, event | category | flops | bytes accessed | tf_op | source)
XLA Modules:
  0.0 22.2 jit_solution(15360545856035801128)
XLA Ops:
  0.0 0.0 copy-start
  0.0 0.0 slice-start
  0.0 3.0 %collective-permute-start = (bf16[32,32,384]{2,1,0:T(8,128)(2,1)}, bf16[32,32,384]{2,1,0:T(8,128)(2,1)S(1)}, u32[]{:S(2)}, u32[]{:S(2)}) collective-permute-start(bf16[32,32,384]{2,1,0:T(8,128)(2,1)} %param.4), channel_id=1, source_target_pairs={{0,16},{4,20},{8,24},{12,28},{16,0},{20,4},{24,8},{28,12},{1,17},{... | collective-permute-start | bytes 2359304 | tf_op jit(solution)/shard_map/ppermute | solution.py:92
  3.6 0.7 %dynamic-slice_convert_fusion = f32[1,2,384]{2,1,0:T(2,128)S(1)} fusion(bf16[360,2,384]{2,1,0:T(2,128)(2,1)} %param.6, s32[]{:T(128)S(6)} %select_n.11), kind=kLoop, calls=%fused_computation.8 | loop fusion | flops 768 | bytes 4612 | tf_op jit(solution)/shard_map/convert_element_type | solution.py:31
  4.3 0.0 slice-done
  4.4 0.0 copy-done
  4.4 0.1 broadcast_maximum_fusion
  4.5 1.6 %fusion.base_ref = f32[1024,384]{1,0:T(8,128)S(1)} fusion(bf16[1024,384]{1,0:T(8,128)(2,1)S(1)} %bitcast.18, bf16[1024,384]{1,0:T(8,128)(2,1)S(1)} %bitcast.19, f32[384]{0:T(512)S(1)} %get-tuple-element.6, f32[384]{0:T(512)S(1)} %get-tuple-element.5, bf16[3,3,384,384]{3,2,1,0:T(8,128)(2,1)} %param.5), kind=kOutput, calls=%fused_computation.1 | convolution fusion | flops 303562752 | bytes 3443712 | tf_op jit(solution)/shard_map/dot_general | solution.py:26
  6.1 14.7 %collective-permute-done = bf16[32,32,384]{2,1,0:T(8,128)(2,1)S(1)} collective-permute-done((bf16[32,32,384]{2,1,0:T(8,128)(2,1)}, bf16[32,32,384]{2,1,0:T(8,128)(2,1)S(1)}, u32[]{:S(2)}, u32[]{:S(2)}) %collective-permute-start) | collective-permute-done | bytes 786464 | tf_op jit(solution)/shard_map/ppermute | solution.py:92
  20.8 1.4 %shard_map.46 = bf16[1024,384]{1,0:T(8,128)(2,1)} custom-call(bf16[1024,384]{1,0:T(8,128)(2,1)S(1)} %bitcast.17, bf16[384,384]{1,0:T(8,128)(2,1)S(1)} %dynamic-slice_bitcast_fusion.tap_ref, f32[1024,384]{1,0:T(8,128)S(1)} %fusion.base_ref, f32[1,384]{1,0:T(1,128)S(1)} %get-tuple-element.7.scale_ref), custom_call_target="tpu_custom_call" | custom-call | flops 301989888 | bytes 3932160 | tf_op jit(solution)/shard_map/pallas_call | solution.py:72
  (2 shorter events, 0.1 us)
Async XLA Ops:
  0.0 4.4 %copy-start = (bf16[32,32,384]{2,1,0:T(8,128)(2,1)S(1)}, bf16[32,32,384]{2,1,0:T(8,128)(2,1)}, u32[]{:S(2)}) copy-start(bf16[32,32,384]{2,1,0:T(8,128)(2,1)} %param.4) | copy-start | bytes 2359300
  0.0 4.3 %slice-start = ((bf16[3,3,384,384]{3,2,1,0:T(8,128)(2,1)}), bf16[3,1,384,384]{3,2,1,0:T(8,128)(2,1)S(1)}, s32[]{:S(2)}) async-start(bf16[3,3,384,384]{3,2,1,0:T(8,128)(2,1)} %param.5), calls=%async_computation | async-start | bytes 1769472 | tf_op jit(solution)/shard_map/slice | solution.py:94
  0.0 20.8 %collective-permute-start = (bf16[32,32,384]{2,1,0:T(8,128)(2,1)}, bf16[32,32,384]{2,1,0:T(8,128)(2,1)S(1)}, u32[]{:S(2)}, u32[]{:S(2)}) collective-permute-start(bf16[32,32,384]{2,1,0:T(8,128)(2,1)} %param.4), channel_id=1, source_target_pairs={{0,16},{4,20},{8,24},{12,28},{16,0},{20,4},{24,8},{28,12},{1,17},{... | collective-permute-start | bytes 2359304 | tf_op jit(solution)/shard_map/ppermute | solution.py:92

commit v7 on v4

--- a/solution.py
+++ b/solution.py
@@ -65,7 +65,7 @@
 
 def finish(other, tap, base, scale):
     cells, chans = base.shape
-    cuts = [cells * eighth // 8 for eighth in (0, 4, 6, 7, 8)]
+    cuts = [cells * part // 16 for part in (0, 4, 8, 12, 14, 15, 16)]
     whole = pl.BlockSpec(memory_space=pltpu.VMEM)
     return pl.pallas_call(
         functools.partial(finish_kernel, cuts),

time: 22.3 us -> 22.3 us (level)
  no operation moved by 1% of the time
where the time goes in v7:
time: 22.3 us; the launch traced here: 22.1 us
  waiting for transfers between devices  14.7 us (66%)
  starting transfers between devices  2.97 us (13%)
  matrix products  1.62 us (7%)
  Pallas kernels  1.32 us (6%)
  other arithmetic  0.78 us (3%)
  between operations  0.7 us (3%)
    ppermute x1, waiting for transfers between devices, paired(): lax.ppermute(encoded, 'rows', [(i, (i + row_step) % count) for i in range...  14.7 us
    ppermute x1, starting transfers between devices, paired(): lax.ppermute(encoded, 'rows', [(i, (i + row_step) % count) for i in range...  2.97 us
    dot_general x1, matrix products, product(): return jnp.dot(flat, tap, preferred_element_type=jnp.float32)  1.62 us
    pallas_call x1, Pallas kernels, finish(): pl.pallas_call(functools.partial(finish_kernel, cuts), out_shape=jax.Shap...  1.32 us
    convert_element_type x1, other arithmetic, film(): chosen = chosen.astype(jnp.float32)  0.69 us
  transfers between devices with their start and end apart: 1, of which 1 were waited for; matrix products, arithmetic and copies ran while one was open for 11% of the time, Pallas kernels for 0%

profile of v7, /device:TPU:0, one launch (start us, length us, event | category | flops | bytes accessed | tf_op | source)
XLA Modules:
  0.0 22.1 jit_solution(10116293549366686555)
XLA Ops:
  0.0 0.0 copy-start
  0.0 0.0 slice-start
  0.0 3.0 %collective-permute-start = (bf16[32,32,384]{2,1,0:T(8,128)(2,1)}, bf16[32,32,384]{2,1,0:T(8,128)(2,1)S(1)}, u32[]{:S(2)}, u32[]{:S(2)}) collective-permute-start(bf16[32,32,384]{2,1,0:T(8,128)(2,1)} %param.4), channel_id=1, source_target_pairs={{0,16},{4,20},{8,24},{12,28},{16,0},{20,4},{24,8},{28,12},{1,17},{... | collective-permute-start | bytes 2359304 | tf_op jit(solution)/shard_map/ppermute | solution.py:90
  3.6 0.7 %dynamic-slice_convert_fusion = f32[1,2,384]{2,1,0:T(2,128)S(1)} fusion(bf16[360,2,384]{2,1,0:T(2,128)(2,1)} %param.6, s32[]{:T(128)S(6)} %select_n.11), kind=kLoop, calls=%fused_computation.8 | loop fusion | flops 768 | bytes 4612 | tf_op jit(solution)/shard_map/convert_element_type | solution.py:31
  4.3 0.0 slice-done
  4.4 0.0 copy-done
  4.4 0.1 broadcast_maximum_fusion
  4.5 1.6 %fusion.base_ref = f32[1024,384]{1,0:T(8,128)S(1)} fusion(bf16[1024,384]{1,0:T(8,128)(2,1)S(1)} %bitcast.18, bf16[1024,384]{1,0:T(8,128)(2,1)S(1)} %bitcast.19, f32[384]{0:T(512)S(1)} %get-tuple-element.6, f32[384]{0:T(512)S(1)} %get-tuple-element.5, bf16[3,3,384,384]{3,2,1,0:T(8,128)(2,1)} %param.5), kind=kOutput, calls=%fused_computation.1 | convolution fusion | flops 303562752 | bytes 3443712 | tf_op jit(solution)/shard_map/dot_general | solution.py:26
  6.1 14.7 %collective-permute-done = bf16[32,32,384]{2,1,0:T(8,128)(2,1)S(1)} collective-permute-done((bf16[32,32,384]{2,1,0:T(8,128)(2,1)}, bf16[32,32,384]{2,1,0:T(8,128)(2,1)S(1)}, u32[]{:S(2)}, u32[]{:S(2)}) %collective-permute-start) | collective-permute-done | bytes 786464 | tf_op jit(solution)/shard_map/ppermute | solution.py:90
  20.8 1.3 %shard_map.46 = bf16[1024,384]{1,0:T(8,128)(2,1)} custom-call(bf16[1024,384]{1,0:T(8,128)(2,1)S(1)} %bitcast.17, bf16[384,384]{1,0:T(8,128)(2,1)S(1)} %dynamic-slice_bitcast_fusion.tap_ref, f32[1024,384]{1,0:T(8,128)S(1)} %fusion.base_ref, f32[1,384]{1,0:T(1,128)S(1)} %get-tuple-element.7.scale_ref), custom_call_target="tpu_custom_call" | custom-call | flops 301989888 | bytes 3932160 | tf_op jit(solution)/shard_map/pallas_call | solution.py:70
  (2 shorter events, 0.1 us)
Async XLA Ops:
  0.0 4.4 %copy-start = (bf16[32,32,384]{2,1,0:T(8,128)(2,1)S(1)}, bf16[32,32,384]{2,1,0:T(8,128)(2,1)}, u32[]{:S(2)}) copy-start(bf16[32,32,384]{2,1,0:T(8,128)(2,1)} %param.4) | copy-start | bytes 2359300
  0.0 4.3 %slice-start = ((bf16[3,3,384,384]{3,2,1,0:T(8,128)(2,1)}), bf16[3,1,384,384]{3,2,1,0:T(8,128)(2,1)S(1)}, s32[]{:S(2)}) async-start(bf16[3,3,384,384]{3,2,1,0:T(8,128)(2,1)} %param.5), calls=%async_computation | async-start | bytes 1769472 | tf_op jit(solution)/shard_map/slice | solution.py:92
  0.0 20.8 %collective-permute-start = (bf16[32,32,384]{2,1,0:T(8,128)(2,1)}, bf16[32,32,384]{2,1,0:T(8,128)(2,1)S(1)}, u32[]{:S(2)}, u32[]{:S(2)}) collective-permute-start(bf16[32,32,384]{2,1,0:T(8,128)(2,1)} %param.4), channel_id=1, source_target_pairs={{0,16},{4,20},{8,24},{12,28},{16,0},{20,4},{24,8},{28,12},{1,17},{... | collective-permute-start | bytes 2359304 | tf_op jit(solution)/shard_map/ppermute | solution.py:90

commit v8 on v7

--- a/solution.py
+++ b/solution.py
@@ -49,18 +49,14 @@
     return (flat + total * scale + beta).astype(jnp.bfloat16).reshape(encoded.shape)
 
 
-def finish_kernel(cuts, other_ref, tap_ref, base_ref, scale_ref, out_ref, stage, sems):
-    copies = []
-    for k, (start, stop) in enumerate(zip(cuts[:-1], cuts[1:])):
+def finish_kernel(cuts, other_ref, tap_ref, base_ref, scale_ref, out_ref, stage, sem):
+    for start, stop in zip(cuts[:-1], cuts[1:]):
         rows = pl.ds(start, stop - start)
         active = jnp.maximum(other_ref[rows, :], jnp.zeros((), jnp.bfloat16))
         part = jnp.dot(active, tap_ref[...], preferred_element_type=jnp.float32)
         stage[rows, :] = (base_ref[rows, :] + part * scale_ref[...]).astype(jnp.bfloat16)
-        copy = pltpu.make_async_copy(stage.at[rows, :], out_ref.at[rows, :], sems.at[k])
-        copy.start()
-        copies.append(copy)
-    for copy in copies:
-        copy.wait()
+        pltpu.make_async_copy(stage.at[rows, :], out_ref.at[rows, :], sem).start()
+    pltpu.make_async_copy(stage, out_ref, sem).wait()
 
 
 def finish(other, tap, base, scale):
@@ -74,7 +70,7 @@
         out_specs=pl.BlockSpec(memory_space=pl.ANY),
         scratch_shapes=[
             pltpu.VMEM((cells, chans), jnp.bfloat16),
-            pltpu.SemaphoreType.DMA((len(cuts) - 1,)),
+            pltpu.SemaphoreType.DMA,
         ],
         compiler_params=pltpu.CompilerParams(vmem_limit_bytes=16 * MIB),
         cost_estimate=pl.CostEstimate(

time: 22.3 us -> 22.2 us (level)
  no operation moved by 1% of the time
where the time goes in v8:
time: 22.2 us; the launch traced here: 22.1 us
  waiting for transfers between devices  14.7 us (66%)
  starting transfers between devices  2.97 us (13%)
  matrix products  1.62 us (7%)
  Pallas kernels  1.27 us (6%)
  other arithmetic  0.78 us (4%)
  between operations  0.7 us (3%)
    ppermute x1, waiting for transfers between devices, paired(): lax.ppermute(encoded, 'rows', [(i, (i + row_step) % count) for i in range...  14.7 us
    ppermute x1, starting transfers between devices, paired(): lax.ppermute(encoded, 'rows', [(i, (i + row_step) % count) for i in range...  2.97 us
    dot_general x1, matrix products, product(): return jnp.dot(flat, tap, preferred_element_type=jnp.float32)  1.62 us
    pallas_call x1, Pallas kernels, finish(): pl.pallas_call(functools.partial(finish_kernel, cuts), out_shape=jax.Shap...  1.27 us
    convert_element_type x1, other arithmetic, film(): chosen = chosen.astype(jnp.float32)  0.69 us
  transfers between devices with their start and end apart: 1, of which 1 were waited for; matrix products, arithmetic and copies ran while one was open for 11% of the time, Pallas kernels for 0%

profile of v8, /device:TPU:0, one launch (start us, length us, event | category | flops | bytes accessed | tf_op | source)
XLA Modules:
  0.0 22.1 jit_solution(5882059641844591628)
XLA Ops:
  0.0 0.0 copy-start
  0.0 0.0 slice-start
  0.0 3.0 %collective-permute-start = (bf16[32,32,384]{2,1,0:T(8,128)(2,1)}, bf16[32,32,384]{2,1,0:T(8,128)(2,1)S(1)}, u32[]{:S(2)}, u32[]{:S(2)}) collective-permute-start(bf16[32,32,384]{2,1,0:T(8,128)(2,1)} %param.4), channel_id=1, source_target_pairs={{0,16},{4,20},{8,24},{12,28},{16,0},{20,4},{24,8},{28,12},{1,17},{... | collective-permute-start | bytes 2359304 | tf_op jit(solution)/shard_map/ppermute | solution.py:86
  3.6 0.7 %dynamic-slice_convert_fusion = f32[1,2,384]{2,1,0:T(2,128)S(1)} fusion(bf16[360,2,384]{2,1,0:T(2,128)(2,1)} %param.6, s32[]{:T(128)S(6)} %select_n.11), kind=kLoop, calls=%fused_computation.8 | loop fusion | flops 768 | bytes 4612 | tf_op jit(solution)/shard_map/convert_element_type | solution.py:31
  4.3 0.0 slice-done
  4.4 0.0 copy-done
  4.4 0.1 broadcast_maximum_fusion
  4.5 1.6 %fusion.base_ref = f32[1024,384]{1,0:T(8,128)S(1)} fusion(bf16[1024,384]{1,0:T(8,128)(2,1)S(1)} %bitcast.18, bf16[1024,384]{1,0:T(8,128)(2,1)S(1)} %bitcast.19, f32[384]{0:T(512)S(1)} %get-tuple-element.6, f32[384]{0:T(512)S(1)} %get-tuple-element.5, bf16[3,3,384,384]{3,2,1,0:T(8,128)(2,1)} %param.5), kind=kOutput, calls=%fused_computation.1 | convolution fusion | flops 303562752 | bytes 3443712 | tf_op jit(solution)/shard_map/dot_general | solution.py:26
  6.1 14.7 %collective-permute-done = bf16[32,32,384]{2,1,0:T(8,128)(2,1)S(1)} collective-permute-done((bf16[32,32,384]{2,1,0:T(8,128)(2,1)}, bf16[32,32,384]{2,1,0:T(8,128)(2,1)S(1)}, u32[]{:S(2)}, u32[]{:S(2)}) %collective-permute-start) | collective-permute-done | bytes 786464 | tf_op jit(solution)/shard_map/ppermute | solution.py:86
  20.8 1.3 %shard_map.46 = bf16[1024,384]{1,0:T(8,128)(2,1)} custom-call(bf16[1024,384]{1,0:T(8,128)(2,1)S(1)} %bitcast.17, bf16[384,384]{1,0:T(8,128)(2,1)S(1)} %dynamic-slice_bitcast_fusion.tap_ref, f32[1024,384]{1,0:T(8,128)S(1)} %fusion.base_ref, f32[1,384]{1,0:T(1,128)S(1)} %get-tuple-element.7.scale_ref), custom_call_target="tpu_custom_call" | custom-call | flops 301989888 | bytes 3932160 | tf_op jit(solution)/shard_map/pallas_call | solution.py:66
  (2 shorter events, 0.1 us)
Async XLA Ops:
  0.0 4.4 %copy-start = (bf16[32,32,384]{2,1,0:T(8,128)(2,1)S(1)}, bf16[32,32,384]{2,1,0:T(8,128)(2,1)}, u32[]{:S(2)}) copy-start(bf16[32,32,384]{2,1,0:T(8,128)(2,1)} %param.4) | copy-start | bytes 2359300
  0.0 4.3 %slice-start = ((bf16[3,3,384,384]{3,2,1,0:T(8,128)(2,1)}), bf16[3,1,384,384]{3,2,1,0:T(8,128)(2,1)S(1)}, s32[]{:S(2)}) async-start(bf16[3,3,384,384]{3,2,1,0:T(8,128)(2,1)} %param.5), calls=%async_computation | async-start | bytes 1769472 | tf_op jit(solution)/shard_map/slice | solution.py:88
  0.0 20.8 %collective-permute-start = (bf16[32,32,384]{2,1,0:T(8,128)(2,1)}, bf16[32,32,384]{2,1,0:T(8,128)(2,1)S(1)}, u32[]{:S(2)}, u32[]{:S(2)}) collective-permute-start(bf16[32,32,384]{2,1,0:T(8,128)(2,1)} %param.4), channel_id=1, source_target_pairs={{0,16},{4,20},{8,24},{12,28},{16,0},{20,4},{24,8},{28,12},{1,17},{... | collective-permute-start | bytes 2359304 | tf_op jit(solution)/shard_map/ppermute | solution.py:86

commit v9 on v8

--- a/solution.py
+++ b/solution.py
@@ -61,7 +61,7 @@
 
 def finish(other, tap, base, scale):
     cells, chans = base.shape
-    cuts = [cells * part // 16 for part in (0, 4, 8, 12, 14, 15, 16)]
+    cuts = [cells * part // 16 for part in (0, 8, 12, 14, 15, 16)]
     whole = pl.BlockSpec(memory_space=pltpu.VMEM)
     return pl.pallas_call(
         functools.partial(finish_kernel, cuts),

time: 22.2 us -> 22.3 us (level)
  no operation moved by 1% of the time
where the time goes in v9:
time: 22.3 us; the launch traced here: 22.1 us
  waiting for transfers between devices  14.7 us (66%)
  starting transfers between devices  2.97 us (13%)
  matrix products  1.62 us (7%)
  Pallas kernels  1.31 us (6%)
  other arithmetic  0.78 us (3%)
  between operations  0.7 us (3%)
    ppermute x1, waiting for transfers between devices, paired(): lax.ppermute(encoded, 'rows', [(i, (i + row_step) % count) for i in range...  14.7 us
    ppermute x1, starting transfers between devices, paired(): lax.ppermute(encoded, 'rows', [(i, (i + row_step) % count) for i in range...  2.97 us
    dot_general x1, matrix products, product(): return jnp.dot(flat, tap, preferred_element_type=jnp.float32)  1.62 us
    pallas_call x1, Pallas kernels, finish(): pl.pallas_call(functools.partial(finish_kernel, cuts), out_shape=jax.Shap...  1.31 us
    convert_element_type x1, other arithmetic, film(): chosen = chosen.astype(jnp.float32)  0.69 us
  transfers between devices with their start and end apart: 1, of which 1 were waited for; matrix products, arithmetic and copies ran while one was open for 11% of the time, Pallas kernels for 0%

profile of v9, /device:TPU:0, one launch (start us, length us, event | category | flops | bytes accessed | tf_op | source)
XLA Modules:
  0.0 22.1 jit_solution(14325668039426639090)
XLA Ops:
  0.0 0.0 copy-start
  0.0 0.0 slice-start
  0.0 3.0 %collective-permute-start = (bf16[32,32,384]{2,1,0:T(8,128)(2,1)}, bf16[32,32,384]{2,1,0:T(8,128)(2,1)S(1)}, u32[]{:S(2)}, u32[]{:S(2)}) collective-permute-start(bf16[32,32,384]{2,1,0:T(8,128)(2,1)} %param.4), channel_id=1, source_target_pairs={{0,16},{4,20},{8,24},{12,28},{16,0},{20,4},{24,8},{28,12},{1,17},{... | collective-permute-start | bytes 2359304 | tf_op jit(solution)/shard_map/ppermute | solution.py:86
  3.6 0.7 %dynamic-slice_convert_fusion = f32[1,2,384]{2,1,0:T(2,128)S(1)} fusion(bf16[360,2,384]{2,1,0:T(2,128)(2,1)} %param.6, s32[]{:T(128)S(6)} %select_n.11), kind=kLoop, calls=%fused_computation.8 | loop fusion | flops 768 | bytes 4612 | tf_op jit(solution)/shard_map/convert_element_type | solution.py:31
  4.3 0.0 slice-done
  4.4 0.0 copy-done
  4.4 0.1 broadcast_maximum_fusion
  4.5 1.6 %fusion.base_ref = f32[1024,384]{1,0:T(8,128)S(1)} fusion(bf16[1024,384]{1,0:T(8,128)(2,1)S(1)} %bitcast.18, bf16[1024,384]{1,0:T(8,128)(2,1)S(1)} %bitcast.19, f32[384]{0:T(512)S(1)} %get-tuple-element.6, f32[384]{0:T(512)S(1)} %get-tuple-element.5, bf16[3,3,384,384]{3,2,1,0:T(8,128)(2,1)} %param.5), kind=kOutput, calls=%fused_computation.1 | convolution fusion | flops 303562752 | bytes 3443712 | tf_op jit(solution)/shard_map/dot_general | solution.py:26
  6.1 14.7 %collective-permute-done = bf16[32,32,384]{2,1,0:T(8,128)(2,1)S(1)} collective-permute-done((bf16[32,32,384]{2,1,0:T(8,128)(2,1)}, bf16[32,32,384]{2,1,0:T(8,128)(2,1)S(1)}, u32[]{:S(2)}, u32[]{:S(2)}) %collective-permute-start) | collective-permute-done | bytes 786464 | tf_op jit(solution)/shard_map/ppermute | solution.py:86
  20.8 1.3 %shard_map.46 = bf16[1024,384]{1,0:T(8,128)(2,1)} custom-call(bf16[1024,384]{1,0:T(8,128)(2,1)S(1)} %bitcast.17, bf16[384,384]{1,0:T(8,128)(2,1)S(1)} %dynamic-slice_bitcast_fusion.tap_ref, f32[1024,384]{1,0:T(8,128)S(1)} %fusion.base_ref, f32[1,384]{1,0:T(1,128)S(1)} %get-tuple-element.7.scale_ref), custom_call_target="tpu_custom_call" | custom-call | flops 301989888 | bytes 3932160 | tf_op jit(solution)/shard_map/pallas_call | solution.py:66
  (2 shorter events, 0.1 us)
Async XLA Ops:
  0.0 4.4 %copy-start = (bf16[32,32,384]{2,1,0:T(8,128)(2,1)S(1)}, bf16[32,32,384]{2,1,0:T(8,128)(2,1)}, u32[]{:S(2)}) copy-start(bf16[32,32,384]{2,1,0:T(8,128)(2,1)} %param.4) | copy-start | bytes 2359300
  0.0 4.3 %slice-start = ((bf16[3,3,384,384]{3,2,1,0:T(8,128)(2,1)}), bf16[3,1,384,384]{3,2,1,0:T(8,128)(2,1)S(1)}, s32[]{:S(2)}) async-start(bf16[3,3,384,384]{3,2,1,0:T(8,128)(2,1)} %param.5), calls=%async_computation | async-start | bytes 1769472 | tf_op jit(solution)/shard_map/slice | solution.py:88
  0.0 20.8 %collective-permute-start = (bf16[32,32,384]{2,1,0:T(8,128)(2,1)}, bf16[32,32,384]{2,1,0:T(8,128)(2,1)S(1)}, u32[]{:S(2)}, u32[]{:S(2)}) collective-permute-start(bf16[32,32,384]{2,1,0:T(8,128)(2,1)} %param.4), channel_id=1, source_target_pairs={{0,16},{4,20},{8,24},{12,28},{16,0},{20,4},{24,8},{28,12},{1,17},{... | collective-permute-start | bytes 2359304 | tf_op jit(solution)/shard_map/ppermute | solution.py:86

commit v10 on v9

--- a/solution.py
+++ b/solution.py
@@ -61,7 +61,7 @@
 
 def finish(other, tap, base, scale):
     cells, chans = base.shape
-    cuts = [cells * part // 16 for part in (0, 8, 12, 14, 15, 16)]
+    cuts = [cells * part // 16 for part in (0, 2, 4, 8, 12, 14, 15, 16)]
     whole = pl.BlockSpec(memory_space=pltpu.VMEM)
     return pl.pallas_call(
         functools.partial(finish_kernel, cuts),

time: 22.3 us -> 22.3 us (level)
  no operation moved by 1% of the time
where the time goes in v10:
time: 22.3 us; the launch traced here: 22.1 us
  waiting for transfers between devices  14.7 us (66%)
  starting transfers between devices  2.97 us (13%)
  matrix products  1.62 us (7%)
  Pallas kernels  1.29 us (6%)
  other arithmetic  0.78 us (3%)
  between operations  0.7 us (3%)
    ppermute x1, waiting for transfers between devices, paired(): lax.ppermute(encoded, 'rows', [(i, (i + row_step) % count) for i in range...  14.7 us
    ppermute x1, starting transfers between devices, paired(): lax.ppermute(encoded, 'rows', [(i, (i + row_step) % count) for i in range...  2.97 us
    dot_general x1, matrix products, product(): return jnp.dot(flat, tap, preferred_element_type=jnp.float32)  1.62 us
    pallas_call x1, Pallas kernels, finish(): pl.pallas_call(functools.partial(finish_kernel, cuts), out_shape=jax.Shap...  1.29 us
    convert_element_type x1, other arithmetic, film(): chosen = chosen.astype(jnp.float32)  0.69 us
  transfers between devices with their start and end apart: 1, of which 1 were waited for; matrix products, arithmetic and copies ran while one was open for 11% of the time, Pallas kernels for 0%

profile of v10, /device:TPU:0, one launch (start us, length us, event | category | flops | bytes accessed | tf_op | source)
XLA Modules:
  0.0 22.1 jit_solution(13487443761476557483)
XLA Ops:
  0.0 0.0 copy-start
  0.0 0.0 slice-start
  0.0 3.0 %collective-permute-start = (bf16[32,32,384]{2,1,0:T(8,128)(2,1)}, bf16[32,32,384]{2,1,0:T(8,128)(2,1)S(1)}, u32[]{:S(2)}, u32[]{:S(2)}) collective-permute-start(bf16[32,32,384]{2,1,0:T(8,128)(2,1)} %param.4), channel_id=1, source_target_pairs={{0,16},{4,20},{8,24},{12,28},{16,0},{20,4},{24,8},{28,12},{1,17},{... | collective-permute-start | bytes 2359304 | tf_op jit(solution)/shard_map/ppermute | solution.py:86
  3.6 0.7 %dynamic-slice_convert_fusion = f32[1,2,384]{2,1,0:T(2,128)S(1)} fusion(bf16[360,2,384]{2,1,0:T(2,128)(2,1)} %param.6, s32[]{:T(128)S(6)} %select_n.11), kind=kLoop, calls=%fused_computation.8 | loop fusion | flops 768 | bytes 4612 | tf_op jit(solution)/shard_map/convert_element_type | solution.py:31
  4.3 0.0 slice-done
  4.4 0.0 copy-done
  4.4 0.1 broadcast_maximum_fusion
  4.5 1.6 %fusion.base_ref = f32[1024,384]{1,0:T(8,128)S(1)} fusion(bf16[1024,384]{1,0:T(8,128)(2,1)S(1)} %bitcast.18, bf16[1024,384]{1,0:T(8,128)(2,1)S(1)} %bitcast.19, f32[384]{0:T(512)S(1)} %get-tuple-element.6, f32[384]{0:T(512)S(1)} %get-tuple-element.5, bf16[3,3,384,384]{3,2,1,0:T(8,128)(2,1)} %param.5), kind=kOutput, calls=%fused_computation.1 | convolution fusion | flops 303562752 | bytes 3443712 | tf_op jit(solution)/shard_map/dot_general | solution.py:26
  6.1 14.7 %collective-permute-done = bf16[32,32,384]{2,1,0:T(8,128)(2,1)S(1)} collective-permute-done((bf16[32,32,384]{2,1,0:T(8,128)(2,1)}, bf16[32,32,384]{2,1,0:T(8,128)(2,1)S(1)}, u32[]{:S(2)}, u32[]{:S(2)}) %collective-permute-start) | collective-permute-done | bytes 786464 | tf_op jit(solution)/shard_map/ppermute | solution.py:86
  20.8 1.3 %shard_map.46 = bf16[1024,384]{1,0:T(8,128)(2,1)} custom-call(bf16[1024,384]{1,0:T(8,128)(2,1)S(1)} %bitcast.17, bf16[384,384]{1,0:T(8,128)(2,1)S(1)} %dynamic-slice_bitcast_fusion.tap_ref, f32[1024,384]{1,0:T(8,128)S(1)} %fusion.base_ref, f32[1,384]{1,0:T(1,128)S(1)} %get-tuple-element.7.scale_ref), custom_call_target="tpu_custom_call" | custom-call | flops 301989888 | bytes 3932160 | tf_op jit(solution)/shard_map/pallas_call | solution.py:66
  (2 shorter events, 0.1 us)
Async XLA Ops:
  0.0 4.4 %copy-start = (bf16[32,32,384]{2,1,0:T(8,128)(2,1)S(1)}, bf16[32,32,384]{2,1,0:T(8,128)(2,1)}, u32[]{:S(2)}) copy-start(bf16[32,32,384]{2,1,0:T(8,128)(2,1)} %param.4) | copy-start | bytes 2359300
  0.0 4.3 %slice-start = ((bf16[3,3,384,384]{3,2,1,0:T(8,128)(2,1)}), bf16[3,1,384,384]{3,2,1,0:T(8,128)(2,1)S(1)}, s32[]{:S(2)}) async-start(bf16[3,3,384,384]{3,2,1,0:T(8,128)(2,1)} %param.5), calls=%async_computation | async-start | bytes 1769472 | tf_op jit(solution)/shard_map/slice | solution.py:88
  0.0 20.8 %collective-permute-start = (bf16[32,32,384]{2,1,0:T(8,128)(2,1)}, bf16[32,32,384]{2,1,0:T(8,128)(2,1)S(1)}, u32[]{:S(2)}, u32[]{:S(2)}) collective-permute-start(bf16[32,32,384]{2,1,0:T(8,128)(2,1)} %param.4), channel_id=1, source_target_pairs={{0,16},{4,20},{8,24},{12,28},{16,0},{20,4},{24,8},{28,12},{1,17},{... | collective-permute-start | bytes 2359304 | tf_op jit(solution)/shard_map/ppermute | solution.py:86

commit v11 on v10

--- a/solution.py
+++ b/solution.py
@@ -61,7 +61,7 @@
 
 def finish(other, tap, base, scale):
     cells, chans = base.shape
-    cuts = [cells * part // 16 for part in (0, 2, 4, 8, 12, 14, 15, 16)]
+    cuts = [cells * part // 16 for part in (0, 4, 8, 12, 15, 16)]
     whole = pl.BlockSpec(memory_space=pltpu.VMEM)
     return pl.pallas_call(
         functools.partial(finish_kernel, cuts),

time: 22.3 us -> 22.2 us (level)
  no operation moved by 1% of the time
where the time goes in v11:
time: 22.2 us; the launch traced here: 22.1 us
  waiting for transfers between devices  14.7 us (66%)
  starting transfers between devices  2.97 us (13%)
  matrix products  1.62 us (7%)
  Pallas kernels  1.28 us (6%)
  other arithmetic  0.78 us (4%)
  between operations  0.7 us (3%)
    ppermute x1, waiting for transfers between devices, paired(): lax.ppermute(encoded, 'rows', [(i, (i + row_step) % count) for i in range...  14.7 us
    ppermute x1, starting transfers between devices, paired(): lax.ppermute(encoded, 'rows', [(i, (i + row_step) % count) for i in range...  2.97 us
    dot_general x1, matrix products, product(): return jnp.dot(flat, tap, preferred_element_type=jnp.float32)  1.62 us
    pallas_call x1, Pallas kernels, finish(): pl.pallas_call(functools.partial(finish_kernel, cuts), out_shape=jax.Shap...  1.28 us
    convert_element_type x1, other arithmetic, film(): chosen = chosen.astype(jnp.float32)  0.69 us
  transfers between devices with their start and end apart: 1, of which 1 were waited for; matrix products, arithmetic and copies ran while one was open for 11% of the time, Pallas kernels for 0%

profile of v11, /device:TPU:0, one launch (start us, length us, event | category | flops | bytes accessed | tf_op | source)
XLA Modules:
  0.0 22.1 jit_solution(3954497434006690317)
XLA Ops:
  0.0 0.0 copy-start
  0.0 0.0 slice-start
  0.0 3.0 %collective-permute-start = (bf16[32,32,384]{2,1,0:T(8,128)(2,1)}, bf16[32,32,384]{2,1,0:T(8,128)(2,1)S(1)}, u32[]{:S(2)}, u32[]{:S(2)}) collective-permute-start(bf16[32,32,384]{2,1,0:T(8,128)(2,1)} %param.4), channel_id=1, source_target_pairs={{0,16},{4,20},{8,24},{12,28},{16,0},{20,4},{24,8},{28,12},{1,17},{... | collective-permute-start | bytes 2359304 | tf_op jit(solution)/shard_map/ppermute | solution.py:86
  3.6 0.7 %dynamic-slice_convert_fusion = f32[1,2,384]{2,1,0:T(2,128)S(1)} fusion(bf16[360,2,384]{2,1,0:T(2,128)(2,1)} %param.6, s32[]{:T(128)S(6)} %select_n.11), kind=kLoop, calls=%fused_computation.8 | loop fusion | flops 768 | bytes 4612 | tf_op jit(solution)/shard_map/convert_element_type | solution.py:31
  4.3 0.0 slice-done
  4.4 0.0 copy-done
  4.4 0.1 broadcast_maximum_fusion
  4.5 1.6 %fusion.base_ref = f32[1024,384]{1,0:T(8,128)S(1)} fusion(bf16[1024,384]{1,0:T(8,128)(2,1)S(1)} %bitcast.18, bf16[1024,384]{1,0:T(8,128)(2,1)S(1)} %bitcast.19, f32[384]{0:T(512)S(1)} %get-tuple-element.6, f32[384]{0:T(512)S(1)} %get-tuple-element.5, bf16[3,3,384,384]{3,2,1,0:T(8,128)(2,1)} %param.5), kind=kOutput, calls=%fused_computation.1 | convolution fusion | flops 303562752 | bytes 3443712 | tf_op jit(solution)/shard_map/dot_general | solution.py:26
  6.1 14.7 %collective-permute-done = bf16[32,32,384]{2,1,0:T(8,128)(2,1)S(1)} collective-permute-done((bf16[32,32,384]{2,1,0:T(8,128)(2,1)}, bf16[32,32,384]{2,1,0:T(8,128)(2,1)S(1)}, u32[]{:S(2)}, u32[]{:S(2)}) %collective-permute-start) | collective-permute-done | bytes 786464 | tf_op jit(solution)/shard_map/ppermute | solution.py:86
  20.8 1.3 %shard_map.46 = bf16[1024,384]{1,0:T(8,128)(2,1)} custom-call(bf16[1024,384]{1,0:T(8,128)(2,1)S(1)} %bitcast.17, bf16[384,384]{1,0:T(8,128)(2,1)S(1)} %dynamic-slice_bitcast_fusion.tap_ref, f32[1024,384]{1,0:T(8,128)S(1)} %fusion.base_ref, f32[1,384]{1,0:T(1,128)S(1)} %get-tuple-element.7.scale_ref), custom_call_target="tpu_custom_call" | custom-call | flops 301989888 | bytes 3932160 | tf_op jit(solution)/shard_map/pallas_call | solution.py:66
  (2 shorter events, 0.1 us)
Async XLA Ops:
  0.0 4.4 %copy-start = (bf16[32,32,384]{2,1,0:T(8,128)(2,1)S(1)}, bf16[32,32,384]{2,1,0:T(8,128)(2,1)}, u32[]{:S(2)}) copy-start(bf16[32,32,384]{2,1,0:T(8,128)(2,1)} %param.4) | copy-start | bytes 2359300
  0.0 4.3 %slice-start = ((bf16[3,3,384,384]{3,2,1,0:T(8,128)(2,1)}), bf16[3,1,384,384]{3,2,1,0:T(8,128)(2,1)S(1)}, s32[]{:S(2)}) async-start(bf16[3,3,384,384]{3,2,1,0:T(8,128)(2,1)} %param.5), calls=%async_computation | async-start | bytes 1769472 | tf_op jit(solution)/shard_map/slice | solution.py:88
  0.0 20.8 %collective-permute-start = (bf16[32,32,384]{2,1,0:T(8,128)(2,1)}, bf16[32,32,384]{2,1,0:T(8,128)(2,1)S(1)}, u32[]{:S(2)}, u32[]{:S(2)}) collective-permute-start(bf16[32,32,384]{2,1,0:T(8,128)(2,1)} %param.4), channel_id=1, source_target_pairs={{0,16},{4,20},{8,24},{12,28},{16,0},{20,4},{24,8},{28,12},{1,17},{... | collective-permute-start | bytes 2359304 | tf_op jit(solution)/shard_map/ppermute | solution.py:86
